TPU v7x, 32 devices: a whole 2x2x4 slice. The times are simulated.
32 devices in a mesh: rep: 4 (over y, x), fsdp: 8 (over z, core).
Axes of the slice: x: 2, y: 2, z: 4, core: 2. Of those that a mesh axis runs over, the one named last changes fastest.
Arguments:
- gate_pre: bfloat16 [2048, 12288], P('rep', 'fsdp'), may hold values from -6 to 6
- up_pre: bfloat16 [2048, 12288], P('rep', 'fsdp'), may hold values from -40 to 40
- out_grad: bfloat16 [2048, 3072], P('rep'), may hold values from -6 to 6
- inner_params: bfloat16 [4, 12288, 3072], P('rep', 'fsdp'), may hold values from -0.109375 to 0.109375
- global_params: float32 [12288, 3072], P('fsdp', 'rep'), may hold values from -0.109375 to 0.109375
- outer_momentum: float32 [12288, 3072], P('fsdp', 'rep'), may hold values from -0.15625 to 0.15625
- pair_codes: int32 [4, 12288, 1536], P('rep', 'fsdp'), may hold values from 0 to 255
- code_scales: float32 [4, 12288, 24], P('rep', 'fsdp'), may hold values from 0.001 to 0.01
Outputs:
- merged_params: bfloat16 [4, 12288, 3072], P('rep', 'fsdp')
- new_global: float32 [12288, 3072], P('fsdp', 'rep')
- new_momentum: float32 [12288, 3072], P('fsdp', 'rep')
Inputs may be any that keep to these rules, and one draw needn't show every extreme that they name: `pair_codes`: each word holds two codes of 0 to 15: its value mod 16 for column 2 j and its value // 16 for column 2 j + 1.
All inputs are finite; a program needn't handle non-finite values.
Results may differ from a plain program's by a relative error of at most 0.011.
Values may be sent and summed in bfloat16 or wider, within the bound.
A program may use at most 128 MiB of HBM per device.

v0:
```python
import jax
import jax.numpy as jnp
from jax import lax
from jax.sharding import PartitionSpec as P


def outer_update(mean_delta, momentum, params):
    new_momentum = 0.9 * momentum + mean_delta
    new_global = params - 0.7 * (mean_delta + 0.9 * new_momentum)
    return (new_momentum, new_global)


def unpack(packed, scales):
    lower_code = packed % 16
    upper_code = packed // 16
    unpacked = jnp.stack([lower_code, upper_code], axis=-1).reshape(
        packed.shape[:-1] + (2 * packed.shape[-1],)
    )
    centered = (unpacked - 8).astype(jnp.float32)
    blocks = centered.reshape(packed.shape[:-1] + (scales.shape[-1], -1)) * scales[..., None]
    return blocks.reshape(unpacked.shape).astype(jnp.bfloat16)


def per_device(
    gate_pre, up_pre, out_grad, inner_params, global_params, outer_momentum, pair_codes, code_scales
):
    replicas = lax.axis_size("rep")
    tok_total = gate_pre.shape[0]
    unit_rows = gate_pre.shape[1]
    model_width = out_grad.shape[1]
    all_units = unit_rows * lax.axis_size("fsdp")
    gate_f32 = gate_pre.astype(jnp.float32)
    upper = up_pre.astype(jnp.float32)
    sigmoid_gate = jax.nn.sigmoid(gate_f32)
    hidden = (gate_f32 * sigmoid_gate * upper).astype(jnp.bfloat16)
    grads = lax.dot_general(
        hidden, out_grad, (((0,), (0,)), ((), ())), preferred_element_type=jnp.float32
    ) * (1.0 / tok_total)
    square_total = lax.psum(jnp.sum(grads * grads), "fsdp")
    root_mean = jnp.sqrt(square_total / (all_units * model_width) + 1e-06)
    clipped = grads * jnp.minimum(1.0, 0.02 / root_mean)
    pseudo = unpack(pair_codes[0], code_scales[0])
    delta_share = lax.psum_scatter(pseudo, "rep", scatter_dimension=1, tiled=True).astype(
        jnp.float32
    ) * (1.0 / replicas)
    new_momentum, new_global = outer_update(delta_share, outer_momentum, global_params)
    global_bf = lax.all_gather(new_global.astype(jnp.bfloat16), "rep", axis=1, tiled=True).astype(
        jnp.float32
    )
    master = inner_params[0].astype(jnp.float32)
    stepped = master - 0.8 * (clipped + 0.2 * master)
    merged_params = (0.5 * stepped + 0.5 * global_bf).astype(jnp.bfloat16)
    return (merged_params[None], new_global, new_momentum)


def solution(mesh):
    in_specs = (
        P("rep", "fsdp"),
        P("rep", "fsdp"),
        P("rep", None),
        P("rep", "fsdp", None),
        P("fsdp", "rep"),
        P("fsdp", "rep"),
        P("rep", "fsdp", None),
        P("rep", "fsdp", None),
    )
    out_specs = (P("rep", "fsdp", None), P("fsdp", "rep"), P("fsdp", "rep"))
    return jax.shard_map(
        per_device, mesh=mesh, in_specs=in_specs, out_specs=out_specs, check_vma=False
    )
```

profile of v0, /device:TPU:0, one launch (start us, length us, event | category | flops | bytes accessed | tf_op | source)
XLA Modules:
  0.0 351.9 jit_solution(9172954984486475729)
XLA Ops:
  7.2 0.0 copy-start
  7.2 0.0 reduce-scatter.2.cloned.1.call-start
  7.2 10.0 %add_select_fusion.1 = (s32[1536,1536,1]{1,0,2:T(8,128)S(1)}, s32[1536,1536,1]{1,0,2:T(8,128)S(1)}) fusion(s32[1,1536,1536]{2,1,0:T(8,128)} %param.14), kind=kLoop, calls=%fused_computation.14 | loop fusion | flops 44826624 | bytes 28311552 | tf_op jit(solution)/shard_map/jit(remainder)/select_n | solution.py:14
  17.2 7.4 %fusion.6 = f32[1536,1536,2]{1,0,2:T(8,128)} fusion(s32[1536,1536,1]{1,0,2:T(8,128)S(1)} %get-tuple-element.7, s32[1536,1536,1]{1,0,2:T(8,128)S(1)} %get-tuple-element.6), kind=kLoop, calls=%fused_computation.10 | loop fusion | flops 14155776 | bytes 37748736 | tf_op jit(solution)/shard_map/convert_element_type | solution.py:19
  24.6 28.5 %copy.13 = f32[1536,1536,2]{0,2,1:T(2,128)} copy(f32[1536,1536,2]{1,0,2:T(8,128)} %fusion.6) | data formatting | bytes 37748736 | tf_op jit(solution)/shard_map/convert_element_type | solution.py:19
  53.1 22.7 %convert_element_type.44 = f32[1536,3072]{0,1:T(8,128)} reshape(f32[1536,1536,2]{0,2,1:T(2,128)} %copy.13) | data formatting | bytes 37748736 | tf_op jit(solution)/shard_map/convert_element_type | solution.py:19
  75.8 0.0 copy-start.2
  75.8 18.7 %copy.15 = f32[1536,3072]{1,0:T(8,128)} copy(f32[1536,3072]{0,1:T(8,128)} %convert_element_type.44) | data formatting | bytes 37748736 | tf_op jit(solution)/shard_map/convert_element_type | solution.py:19
  94.5 0.0 copy-done.2
  94.5 1.2 copy.14
  95.7 0.0 copy-start.1
  95.7 10.6 %mul.83 = f32[1536,24,128]{2,1,0:T(8,128)} broadcast(f32[1536,24]{1,0:T(8,128)} %copy.14), dimensions={0,1} | broadcast | bytes 19021824 | tf_op jit(solution)/shard_map/mul | solution.py:20
  106.2 2.6 copy-done.1
  108.8 14.3 %fusion.5 = bf16[1536,3072]{1,0:T(8,128)(2,1)} fusion(f32[1536,3072]{1,0:T(8,128)S(1)} %copy-done.1, f32[192,8,24,128]{3,2,1,0:T(8,128)} %bitcast.40), kind=kLoop, calls=%fused_computation.8 | loop fusion | flops 9437184 | bytes 47185920 | tf_op jit(solution)/shard_map/convert_element_type | solution.py:21
  123.1 0.0 reduce-scatter.2.cloned.1.call-update
  123.1 0.2 all-gather.2.cloned.1.call-start
  123.4 97.6 %reduce-scatter.2.cloned.1.call-done = bf16[1536,768]{1,0:T(8,128)(2,1)} async-done(((bf16[1536,3072]{1,0:T(8,128)(2,1)}), bf16[1536,768]{1,0:T(8,128)(2,1)}) %reduce-scatter.2.cloned.1.call-update) | async-done | bytes 2359312 | tf_op jit(solution)/shard_map/reduce_scatter | solution.py:43
  221.0 10.2 %fusion.20 = (bf16[1536,768]{1,0:T(8,128)(2,1)}, f32[1536,768]{1,0:T(8,128)}, f32[1536,768]{1,0:T(8,128)}) fusion(f32[1536,768]{1,0:T(8,128)} %param.12, bf16[1536,768]{1,0:T(8,128)(2,1)} %reduce-scatter.2.cloned.1.call-done, f32[1536,768]{1,0:T(8,128)} %param.13), kind=kLoop, calls=%fused_computation.36 | loop fusion | flops 10616832 | bytes 23592960 | tf_op jit(solution)/shard_map/convert_element_type | solution.py:47
  231.1 0.0 all-gather.2.cloned.1.call-update
  231.1 0.0 copy-done
  231.2 14.2 %multiply_reduce_fusion = (f32[]{:T(128)}, f32[1536,3072]{1,0:T(8,128)}) fusion(bf16[512,3072]{1,0:T(8,128)(2,1)S(1)} %copy-done, bf16[512,1536]{1,0:T(8,128)(2,1)} %param.9, bf16[512,1536]{1,0:T(8,128)(2,1)} %param.8), kind=kOutput, calls=%fused_computation.11 | convolution fusion | flops 4852285440 | bytes 25165828 | tf_op jit(solution)/shard_map/dot_general | solution.py:36
  245.3 17.0 %psum.7 = f32[]{:T(128)} all-reduce(f32[]{:T(128)} %get-tuple-element.8), channel_id=1, replica_groups=mesh['rep'=4,'fsdp'=8] {'fsdp'}, use_global_device_ids=true, to_apply=%region_1.0 | all-reduce | flops 1 | bytes 8 | tf_op jit(solution)/shard_map/psum | solution.py:39
  263.0 64.7 %all-gather.2.cloned.1.call-done = bf16[1536,3072]{1,0:T(8,128)(2,1)} async-done(((bf16[1536,768]{1,0:T(8,128)(2,1)}), bf16[1536,3072]{1,0:T(8,128)(2,1)}) %all-gather.2.cloned.1.call-update) | async-done | bytes 9437200 | tf_op jit(solution)/shard_map/all_gather | solution.py:47
  327.7 17.4 %fusion.7 = bf16[1,1536,3072]{2,1,0:T(8,128)(2,1)} fusion(bf16[1536,3072]{1,0:T(8,128)(2,1)} %all-gather.2.cloned.1.call-done, f32[1536,3072]{1,0:T(8,128)} %get-tuple-element.9, bf16[1,1536,3072]{2,1,0:T(8,128)(2,1)} %param.11, f32[]{:T(128)S(6)} %mul.75), kind=kLoop, calls=%fused_computation.17 | loop fusion | flops 47185920 | bytes 47185924 | tf_op jit(solution)/shard_map/broadcast_in_dim | solution.py:53
Async XLA Ops:
  7.2 224.0 %copy-start = (bf16[512,3072]{1,0:T(8,128)(2,1)S(1)}, bf16[512,3072]{1,0:T(8,128)(2,1)}, u32[]{:S(2)}) copy-start(bf16[512,3072]{1,0:T(8,128)(2,1)} %param.10) | copy-start | bytes 9437188
  7.2 213.8 %reduce-scatter.2.cloned.1.call-start = ((), (), s32[]{:S(2)}) async-start(), calls=%async_computation.1 | async-start | bytes 11796480 | tf_op jit(solution)/shard_map/reduce_scatter | solution.py:43
  75.8 18.7 %copy-start.2 = (f32[1,1536,24]{1,2,0:T(8,128)S(1)}, f32[1,1536,24]{1,2,0:T(8,128)}, u32[]{:S(2)}) copy-start(f32[1,1536,24]{1,2,0:T(8,128)} %param.15) | copy-start | bytes 442372
  95.7 13.1 %copy-start.1 = (f32[1536,3072]{1,0:T(8,128)S(1)}, f32[1536,3072]{1,0:T(8,128)}, u32[]{:S(2)}) copy-start(f32[1536,3072]{1,0:T(8,128)} %copy.15) | copy-start | bytes 56623108
  123.1 204.5 %all-gather.2.cloned.1.call-start = ((), (), s32[]{:S(2)}) async-start(), calls=%async_computation.2 | async-start | bytes 11796480 | tf_op jit(solution)/shard_map/all_gather | solution.py:47
Sparse Core Ops, SparseCore 0:
  123.3 97.6 reduce-scatter.1
  231.3 96.3 all-gather.1
where the time goes:
time: 354 us; the launch traced here: 352 us
  waiting for transfers between devices  162 us (46%)
  local copies, waits for them, and re-layouts  84.2 us (24%)
  other arithmetic  59.3 us (17%)
  blocking collectives  17 us (5%)
  between operations  14.7 us (4%)
  matrix products  14.2 us (4%)
    reduce_scatter x1, waiting for transfers between devices, per_device(): lax.psum_scatter(pseudo, 'rep', scatter_dimension=1, tiled=True)  97.6 us
    convert_element_type x3, local copies, waits for them, and re-layouts, unpack(): centered = (unpacked - 8).astype(jnp.float32)  69.8 us
    all_gather x1, waiting for transfers between devices, per_device(): lax.all_gather(new_global.astype(jnp.bfloat16), 'rep', axis=1, tiled=True)  64.7 us
    broadcast_in_dim x1, other arithmetic, per_device(): return (merged_params[None], new_global, new_momentum)  17.4 us
    psum x1, blocking collectives, per_device(): square_total = lax.psum(jnp.sum(grads * grads), 'fsdp')  17 us
    convert_element_type x1, other arithmetic, unpack(): return blocks.reshape(unpacked.shape).astype(jnp.bfloat16)  14.3 us
    dot_general x1, matrix products, per_device(): lax.dot_general(hidden, out_grad, (((0,), (0,)), ((), ())), preferred_ele...  14.2 us
    mul x2, local copies, waits for them, and re-layouts, unpack(): centered.reshape(packed.shape[:-1] + (scales.shape[-1], -1))  11.7 us
  transfers between devices with their start and end apart: 2, of which 2 were waited for; matrix products, arithmetic and copies ran while one was open for 4% of the time, Pallas kernels for 0%

commit v1 on v0

--- a/solution.py
+++ b/solution.py
@@ -1,6 +1,9 @@
+import functools
 import jax
 import jax.numpy as jnp
 from jax import lax
+from jax.experimental import pallas as pl
+from jax.experimental.pallas import tpu as pltpu
 from jax.sharding import PartitionSpec as P
 
 
@@ -21,7 +24,7 @@
     return blocks.reshape(unpacked.shape).astype(jnp.bfloat16)
 
 
-def per_device(
+def per_device_any(
     gate_pre, up_pre, out_grad, inner_params, global_params, outer_momentum, pair_codes, code_scales
 ):
     replicas = lax.axis_size("rep")
@@ -53,6 +56,360 @@
     return (merged_params[None], new_global, new_momentum)
 
 
+SLOTS = 4
+MESH = pl.DeviceIdType.MESH
+
+
+def fused_step(
+    chunk, shards, tok_total, all_entries,
+    gate, up, og, inner, glob, mom, codes, scales,
+    merged_out, glob_out, mom_out,
+    pseudo, ra, rb, sa, sb, r2a, r2b, gbf, glob_v, mom_v, code_v, scale_v,
+    gate_v, up_v, og_v, hid_t, inner_v, merged_v, spread, squares, sums, factor,
+    send_sem, recv_sem, sum_send, sum_recv, code_sem, load_sem, inner_sem, merged_sem, out_sem,
+):
+    rows = glob_v.shape[0]
+    quarter = glob_v.shape[1]
+    half = chunk // 2
+    count = rows // chunk
+    rep = lax.axis_index("rep")
+    shard = lax.axis_index("fsdp")
+    y, x = rep // 2, rep % 2
+    x_peer, y_peer = y * 2 + (1 - x), (1 - y) * 2 + x
+
+    def whole(c):
+        return pl.ds(pl.multiple_of(c * chunk, chunk), chunk)
+
+    def first(c):
+        return pl.ds(pl.multiple_of(c * chunk, half), half)
+
+    def second(c):
+        return pl.ds(pl.multiple_of(c * chunk + half, half), half)
+
+    def packed(c):
+        return pl.ds(pl.multiple_of(c * half, half), half)
+
+    def remote(src, dst, kind, c, peer):
+        return pltpu.make_async_remote_copy(
+            src_ref=src, dst_ref=dst, send_sem=send_sem.at[kind, c], recv_sem=recv_sem.at[kind, c],
+            device_id=(peer, shard), device_id_type=MESH,
+        )
+
+    def scatter_x(c):
+        return remote(pseudo.at[:, 1 - x, first(c)], ra.at[:, packed(c)], 0, c, x_peer)
+
+    def scatter_y(c):
+        return remote(pseudo.at[1 - y, :, second(c)], rb.at[:, packed(c)], 1, c, y_peer)
+
+    def pass_y(c):
+        return remote(sa.at[packed(c)], r2a.at[packed(c)], 2, c, y_peer)
+
+    def pass_x(c):
+        return remote(sb.at[packed(c)], r2b.at[packed(c)], 3, c, x_peer)
+
+    def own_x(c, at_x):
+        block = gbf.at[y, at_x, whole(c)]
+        return remote(block, block, 4, c, x_peer)
+
+    def own_y(c, at_y):
+        block = gbf.at[at_y, x, whole(c)]
+        return remote(block, block, 5, c, y_peer)
+
+    def onward_x(c, at_x):
+        block = gbf.at[1 - y, at_x, first(c)]
+        return remote(block, block, 6, c, x_peer)
+
+    def onward_y(c, at_y):
+        block = gbf.at[at_y, 1 - x, second(c)]
+        return remote(block, block, 7, c, y_peer)
+
+    def sum_copy(step):
+        return pltpu.make_async_remote_copy(
+            src_ref=sums.at[0], dst_ref=sums.at[step],
+            send_sem=sum_send.at[step - 1], recv_sem=sum_recv.at[step - 1],
+            device_id=(rep, (shard + step) % shards), device_id_type=MESH,
+        )
+
+    def code_copy(c):
+        return pltpu.make_async_copy(
+            codes.at[whole(c)], code_v.at[c % SLOTS], code_sem.at[c % SLOTS]
+        )
+
+    def inner_copy(c):
+        return pltpu.make_async_copy(inner.at[whole(c)], inner_v.at[c % 2], inner_sem.at[c % 2])
+
+    def merged_copy(c):
+        return pltpu.make_async_copy(
+            merged_v.at[c % 2], merged_out.at[whole(c)], merged_sem.at[c % 2]
+        )
+
+    def glob_copy(c):
+        return pltpu.make_async_copy(glob_v.at[whole(c)], glob_out.at[whole(c)], out_sem.at[0, c])
+
+    def mom_copy(c):
+        return pltpu.make_async_copy(mom_v.at[whole(c)], mom_out.at[whole(c)], out_sem.at[1, c])
+
+    barrier = pltpu.get_barrier_semaphore()
+    for peer in (x_peer, y_peer):
+        pl.semaphore_signal(barrier, inc=1, device_id=(peer, shard), device_id_type=MESH)
+    for step in range(1, shards):
+        pl.semaphore_signal(
+            barrier, inc=1, device_id=(rep, (shard + step) % shards), device_id_type=MESH
+        )
+
+    scale_load = pltpu.make_async_copy(scales, scale_v, load_sem.at[0])
+    gate_load = pltpu.make_async_copy(gate, gate_v, load_sem.at[1])
+    up_load = pltpu.make_async_copy(up, up_v, load_sem.at[2])
+    og_load = pltpu.make_async_copy(og, og_v, load_sem.at[3])
+    glob_load = pltpu.make_async_copy(glob, glob_v, load_sem.at[4])
+    mom_load = pltpu.make_async_copy(mom, mom_v, load_sem.at[5])
+    scale_load.start()
+    for c in range(min(SLOTS, count)):
+        code_copy(c).start()
+    for load in (gate_load, up_load, og_load, glob_load, mom_load):
+        load.start()
+    for c in range(min(2, count)):
+        inner_copy(c).start()
+
+    k = lax.broadcasted_iota(jnp.int32, (256, 256), 0)
+    n = lax.broadcasted_iota(jnp.int32, (256, 256), 1)
+    j, odd = n >> 1, n & 1
+    from_word = jnp.where((k == j) & (odd == 0), 1.0, 0.0)
+    from_upper = jnp.where(k == j + 128, jnp.where(odd == 0, -16.0, 1.0), 0.0)
+    spread[...] = (from_word + from_upper).astype(jnp.bfloat16)
+    squares[...] = jnp.zeros_like(squares)
+
+    scale_load.wait()
+    pl.semaphore_wait(barrier, shards + 1)
+
+    def unpack_chunk(c, carry):
+        code_copy(c).wait()
+        slot = c % SLOTS
+        for b in range(code_v.shape[2] // 128):
+            word = code_v[slot, :, 128 * b : 128 * b + 128]
+            pair = jnp.concatenate(
+                [
+                    (word - 136).astype(jnp.float32).astype(jnp.bfloat16),
+                    ((word >> 4) - 8).astype(jnp.float32).astype(jnp.bfloat16),
+                ],
+                axis=1,
+            )
+            centered = jnp.dot(pair, spread[...], preferred_element_type=jnp.float32)
+            for part in range(2):
+                col = 256 * b + 128 * part
+                q, at = col // quarter, col % quarter
+                value = centered[:, 128 * part : 128 * part + 128]
+                value = value * scale_v[whole(c), 2 * b + part : 2 * b + part + 1]
+                pseudo[q // 2, q % 2, whole(c), at : at + 128] = value.astype(jnp.bfloat16)
+        scatter_x(c).start()
+        scatter_y(c).start()
+
+        @pl.when(c + SLOTS < count)
+        def _():
+            code_copy(c + SLOTS).start()
+
+        return carry
+
+    lax.fori_loop(0, count, unpack_chunk, 0)
+
+    gate_load.wait()
+    up_load.wait()
+    og_load.wait()
+
+    def square_chunk(c, carry):
+        cols = whole(c)
+        g = gate_v[:, cols].astype(jnp.float32)
+        h = g * jax.nn.sigmoid(g) * up_v[:, cols].astype(jnp.float32)
+        hid_t[cols, :] = h.T.astype(jnp.bfloat16)
+        for q in range(4):
+            grad = jnp.dot(
+                hid_t[cols, :], og_v[:, quarter * q : quarter * (q + 1)],
+                preferred_element_type=jnp.float32,
+            ) * (1.0 / tok_total)
+            squares[...] += jnp.sum((grad * grad).reshape(chunk // 8, 8, quarter), axis=0)
+        return carry
+
+    lax.fori_loop(0, count, square_chunk, 0)
+    sums[0] = jnp.full((8, 128), jnp.sum(squares[...]), jnp.float32)
+    for step in range(1, shards):
+        sum_copy(step).start()
+
+    def pass_chunk(c, carry):
+        scatter_x(c).wait_recv()
+        mine = pseudo[1 - y, x, first(c)].astype(jnp.float32)
+        sa[packed(c)] = (mine + ra[1 - y, packed(c)].astype(jnp.float32)).astype(jnp.bfloat16)
+        pass_y(c).start()
+        scatter_y(c).wait_recv()
+        mine = pseudo[y, 1 - x, second(c)].astype(jnp.float32)
+        sb[packed(c)] = (mine + rb[1 - x, packed(c)].astype(jnp.float32)).astype(jnp.bfloat16)
+        pass_x(c).start()
+        return carry
+
+    lax.fori_loop(0, count, pass_chunk, 0)
+    glob_load.wait()
+    mom_load.wait()
+
+    def outer_rows(at, total):
+        new_momentum, new_global = outer_update(total * 0.25, mom_v[at], glob_v[at])
+        mom_v[at] = new_momentum
+        glob_v[at] = new_global
+        gbf[y, x, at] = new_global.astype(jnp.bfloat16)
+
+    def outer_chunk(c, carry):
+        f32 = jnp.float32
+        pass_y(c).wait_recv()
+        at, near = first(c), packed(c)
+        outer_rows(at, pseudo[y, x, at].astype(f32) + ra[y, near].astype(f32) + r2a[near].astype(f32))
+        pass_x(c).wait_recv()
+        at = second(c)
+        outer_rows(at, pseudo[y, x, at].astype(f32) + rb[x, near].astype(f32) + r2b[near].astype(f32))
+        own_x(c, x).start()
+        own_y(c, y).start()
+        glob_copy(c).start()
+        mom_copy(c).start()
+        return carry
+
+    lax.fori_loop(0, count, outer_chunk, 0)
+
+    for step in range(1, shards):
+        sum_copy(step).wait_recv()
+    total = sums[0]
+    for step in range(1, shards):
+        total = total + sums[step]
+    root_mean = jnp.sqrt(total / all_entries + 1e-06)
+    scale = jnp.minimum(1.0, 0.02 / root_mean) * (0.4 / tok_total)
+    factor[...] = jnp.concatenate([scale] * (quarter // 128), axis=1)
+
+    def onward_chunk(c, carry):
+        own_y(c, 1 - y).wait_recv()
+        onward_x(c, x).start()
+        own_x(c, 1 - x).wait_recv()
+        onward_y(c, y).start()
+        return carry
+
+    lax.fori_loop(0, count, onward_chunk, 0)
+
+    def merge_chunk(c, carry):
+        slot = c % 2
+        inner_copy(c).wait()
+
+        @pl.when(c >= 2)
+        def _():
+            merged_copy(c - 2).wait()
+
+        onward_x(c, 1 - x).wait_recv()
+        onward_y(c, 1 - y).wait_recv()
+        for q in range(4):
+            cols = slice(quarter * q, quarter * (q + 1))
+            grad = jnp.dot(hid_t[whole(c), :], og_v[:, cols], preferred_element_type=jnp.float32)
+            kept = 0.42 * inner_v[slot, :, cols].astype(jnp.float32)
+            kept = kept + 0.5 * gbf[q // 2, q % 2, whole(c)].astype(jnp.float32)
+            merged_v[slot, :, cols] = (kept - grad * factor[0:1, :]).astype(jnp.bfloat16)
+        merged_copy(c).start()
+
+        @pl.when(c + 2 < count)
+        def _():
+            inner_copy(c + 2).start()
+
+        return carry
+
+    lax.fori_loop(0, count, merge_chunk, 0)
+    for c in range(max(count - 2, 0), count):
+        merged_copy(c).wait()
+
+    def drain(c, carry):
+        scatter_x(c).wait_send()
+        scatter_y(c).wait_send()
+        pass_y(c).wait_send()
+        pass_x(c).wait_send()
+        own_x(c, x).wait_send()
+        own_y(c, y).wait_send()
+        onward_x(c, x).wait_send()
+        onward_y(c, y).wait_send()
+        glob_copy(c).wait()
+        mom_copy(c).wait()
+        return carry
+
+    lax.fori_loop(0, count, drain, 0)
+    for step in range(1, shards):
+        sum_copy(step).wait_send()
+
+
+def per_device_square(
+    gate_pre, up_pre, out_grad, inner_params, global_params, outer_momentum, pair_codes, code_scales
+):
+    shards = lax.axis_size("fsdp")
+    tokens, rows = gate_pre.shape
+    width = out_grad.shape[1]
+    quarter = width // 4
+    chunk = 128
+    count = rows // chunk
+    bf16, f32 = jnp.bfloat16, jnp.float32
+    dma = pltpu.SemaphoreType.DMA
+    any_spec = pl.BlockSpec(memory_space=pl.ANY)
+    merged, new_global, new_momentum = pl.pallas_call(
+        functools.partial(fused_step, chunk, shards, tokens, rows * shards * width),
+        out_shape=(
+            jax.ShapeDtypeStruct((rows, width), bf16),
+            jax.ShapeDtypeStruct((rows, quarter), f32),
+            jax.ShapeDtypeStruct((rows, quarter), f32),
+        ),
+        in_specs=[any_spec] * 8,
+        out_specs=(any_spec,) * 3,
+        scratch_shapes=[
+            pltpu.VMEM((2, 2, rows, quarter), bf16),
+            pltpu.VMEM((2, rows // 2, quarter), bf16),
+            pltpu.VMEM((2, rows // 2, quarter), bf16),
+            pltpu.VMEM((rows // 2, quarter), bf16),
+            pltpu.VMEM((rows // 2, quarter), bf16),
+            pltpu.VMEM((rows // 2, quarter), bf16),
+            pltpu.VMEM((rows // 2, quarter), bf16),
+            pltpu.VMEM((2, 2, rows, quarter), bf16),
+            pltpu.VMEM((rows, quarter), f32),
+            pltpu.VMEM((rows, quarter), f32),
+            pltpu.VMEM((SLOTS, chunk, width // 2), jnp.int32),
+            pltpu.VMEM(code_scales.shape[1:], f32),
+            pltpu.VMEM((tokens, rows), bf16),
+            pltpu.VMEM((tokens, rows), bf16),
+            pltpu.VMEM((tokens, width), bf16),
+            pltpu.VMEM((rows, tokens), bf16),
+            pltpu.VMEM((2, chunk, width), bf16),
+            pltpu.VMEM((2, chunk, width), bf16),
+            pltpu.VMEM((256, 256), bf16),
+            pltpu.VMEM((8, quarter), f32),
+            pltpu.VMEM((shards, 8, 128), f32),
+            pltpu.VMEM((8, quarter), f32),
+            dma((8, count)),
+            dma((8, count)),
+            dma((shards - 1,)),
+            dma((shards - 1,)),
+            dma((SLOTS,)),
+            dma((6,)),
+            dma((2,)),
+            dma((2,)),
+            dma((2, count)),
+        ],
+        compiler_params=pltpu.CompilerParams(
+            collective_id=0, has_side_effects=True, vmem_limit_bytes=60 * 1024 * 1024
+        ),
+        cost_estimate=pl.CostEstimate(
+            flops=4 * tokens * rows * width, bytes_accessed=22 * rows * width, transcendentals=0
+        ),
+    )(
+        gate_pre, up_pre, out_grad, inner_params[0], global_params, outer_momentum,
+        pair_codes[0], code_scales[0],
+    )
+    return (merged[None], new_global, new_momentum)
+
+
+def per_device(*arrays):
+    rows, width = arrays[0].shape[1], arrays[2].shape[1]
+    square = lax.axis_size("rep") == 4 and lax.axis_size("fsdp") > 1
+    if square and rows % 128 == 0 and width % 1024 == 0 and width // arrays[7].shape[2] == 128:
+        return per_device_square(*arrays)
+    return per_device_any(*arrays)
+
+
 def solution(mesh):
     in_specs = (
         P("rep", "fsdp"),

time: 354 us -> 182 us (0.51)
  Pallas kernels: 0 us -> 164 us
  waiting for transfers between devices: 162 us -> 0 us
  local copies, waits for them, and re-layouts: 84.2 us -> 17.5 us
  other arithmetic: 59.3 us -> 0 us
  blocking collectives: 17 us -> 0 us
  matrix products: 14.2 us -> 0 us
  between operations: 14.7 us -> 0.64 us
    pallas_call x0 -> x1, Pallas kernels: none -> 164 us  [per_device_square(): pl.pallas_call(functools.partial(fused_step, chunk, shards, tokens, rows...]
    reduce_scatter x1 -> x0, waiting for transfers between devices: 97.6 us -> none  [per_device(): lax.psum_scatter(pseudo, 'rep', scatter_dimension=1, tiled=True)]
    convert_element_type x3 -> x0, local copies, waits for them, and re-layouts: 69.8 us -> none  [unpack(): centered = (unpacked - 8).astype(jnp.float32)]
    all_gather x1 -> x0, waiting for transfers between devices: 64.7 us -> none  [per_device(): lax.all_gather(new_global.astype(jnp.bfloat16), 'rep', axis=1, tiled=True)]
    convert_element_type x3 -> x0, other arithmetic: 31.9 us -> none  [the longest x1 14.3 us: unpack(): return blocks.reshape(unpacked.shape).astype(jnp.bfloat16)]
    broadcast_in_dim x1 -> x0, other arithmetic: 17.4 us -> none  [per_device(): return (merged_params[None], new_global, new_momentum)]
    psum x1 -> x0, blocking collectives: 17 us -> none  [per_device(): square_total = lax.psum(jnp.sum(grads * grads), 'fsdp')]
    unnamed x6, local copies, waits for them, and re-layouts: 2.57 us -> 17.5 us
  transfers between devices with their start and end apart: 2 -> 0, of which waited for: 2 -> 0; matrix products, arithmetic and copies ran while one was open for 4% -> 0% of each run, Pallas kernels for 0% -> 0%
where the time goes in v1:
time: 182 us
  Pallas kernels  164 us (90%)
  local copies, waits for them, and re-layouts  17.5 us (10%)
    pallas_call x1, Pallas kernels, per_device_square(): pl.pallas_call(functools.partial(fused_step, chunk, shards, tokens, rows...  164 us
    unnamed x6, local copies, waits for them, and re-layouts  17.5 us

profile of v1, /device:TPU:0, one launch (start us, length us, event | category | flops | bytes accessed | tf_op | source)
XLA Modules:
  0.0 181.9 jit_solution(14633543796103516434)
XLA Ops:
  0.6 2.1 %copy.11 = f32[1,1536,24]{2,1,0:T(8,128)} copy(f32[1,1536,24]{1,2,0:T(8,128)} %param.15) | data formatting | bytes 294912 | tf_op args[7]
  2.7 163.8 %shard_map.103 = (bf16[1536,3072]{1,0:T(8,128)(2,1)}, f32[1536,768]{1,0:T(8,128)}, f32[1536,768]{1,0:T(8,128)}) custom-call(bf16[512,1536]{1,0:T(8,128)(2,1)} %gate.1, bf16[512,1536]{1,0:T(8,128)(2,1)} %up.1, bf16[512,3072]{1,0:T(8,128)(2,1)} %og.1, bf16[1536,3072]{1,0:T(8,128)(2,1)} %bitcast.6, f32[1536,768]{1,0:T(8,128)} %glob.1, f32[1536,768]{1,0:T(8,128)} %mom.1, ...), custom_call_target="tpu_custom_call" | custom-call | flops 9663676416 | bytes 103809024 | tf_op jit(solution)/shard_map/pallas_call | solution.py:350
  166.5 8.3 %copy.15 = bf16[1,1536,3072]{2,1,0:T(8,128)(2,1)} copy(bf16[1,1536,3072]{2,1,0:T(8,128)(2,1)} %bitcast.4) | data formatting | bytes 18874368
  174.8 0.0 copy-start
  174.8 5.0 %copy.16 = f32[1536,768]{1,0:T(8,128)} copy(f32[1536,768]{1,0:T(8,128)} %get-tuple-element.13) | data formatting | bytes 9437184
  179.8 0.0 copy-done
  179.8 2.2 %copy.17 = f32[1536,768]{1,0:T(8,128)} copy(f32[1536,768]{1,0:T(8,128)S(1)} %copy-done) | data formatting | bytes 9437184
Async XLA Ops:
  174.8 5.0 %copy-start = (f32[1536,768]{1,0:T(8,128)S(1)}, f32[1536,768]{1,0:T(8,128)}, u32[]{:S(2)}) copy-start(f32[1536,768]{1,0:T(8,128)} %get-tuple-element.14) | copy-start | bytes 14155780

commit v2 on v1

--- a/solution.py
+++ b/solution.py
@@ -63,10 +63,10 @@
 def fused_step(
     chunk, shards, tok_total, all_entries,
     gate, up, og, inner, glob, mom, codes, scales,
-    merged_out, glob_out, mom_out,
-    pseudo, ra, rb, sa, sb, r2a, r2b, gbf, glob_v, mom_v, code_v, scale_v,
-    gate_v, up_v, og_v, hid_t, inner_v, merged_v, spread, squares, sums, factor,
-    send_sem, recv_sem, sum_send, sum_recv, code_sem, load_sem, inner_sem, merged_sem, out_sem,
+    pseudo, glob_v, mom_v,
+    ra, rb, sa, sb, r2a, r2b, gbf, code_v, scale_v,
+    gate_v, up_v, og_v, hid_t, inner_v, spread, squares, sums, factor,
+    send_sem, recv_sem, sum_send, sum_recv, code_sem, load_sem, inner_sem,
 ):
     rows = glob_v.shape[0]
     quarter = glob_v.shape[1]
@@ -137,17 +137,6 @@
 
     def inner_copy(c):
         return pltpu.make_async_copy(inner.at[whole(c)], inner_v.at[c % 2], inner_sem.at[c % 2])
-
-    def merged_copy(c):
-        return pltpu.make_async_copy(
-            merged_v.at[c % 2], merged_out.at[whole(c)], merged_sem.at[c % 2]
-        )
-
-    def glob_copy(c):
-        return pltpu.make_async_copy(glob_v.at[whole(c)], glob_out.at[whole(c)], out_sem.at[0, c])
-
-    def mom_copy(c):
-        return pltpu.make_async_copy(mom_v.at[whole(c)], mom_out.at[whole(c)], out_sem.at[1, c])
 
     barrier = pltpu.get_barrier_semaphore()
     for peer in (x_peer, y_peer):
@@ -184,6 +173,7 @@
 
     def unpack_chunk(c, carry):
         code_copy(c).wait()
+        block_scale = scale_v[:, whole(c)].T
         slot = c % SLOTS
         for b in range(code_v.shape[2] // 128):
             word = code_v[slot, :, 128 * b : 128 * b + 128]
@@ -199,7 +189,7 @@
                 col = 256 * b + 128 * part
                 q, at = col // quarter, col % quarter
                 value = centered[:, 128 * part : 128 * part + 128]
-                value = value * scale_v[whole(c), 2 * b + part : 2 * b + part + 1]
+                value = value * block_scale[:, 2 * b + part : 2 * b + part + 1]
                 pseudo[q // 2, q % 2, whole(c), at : at + 128] = value.astype(jnp.bfloat16)
         scatter_x(c).start()
         scatter_y(c).start()
@@ -265,8 +255,6 @@
         outer_rows(at, pseudo[y, x, at].astype(f32) + rb[x, near].astype(f32) + r2b[near].astype(f32))
         own_x(c, x).start()
         own_y(c, y).start()
-        glob_copy(c).start()
-        mom_copy(c).start()
         return carry
 
     lax.fori_loop(0, count, outer_chunk, 0)
@@ -293,10 +281,8 @@
         slot = c % 2
         inner_copy(c).wait()
 
-        @pl.when(c >= 2)
-        def _():
-            merged_copy(c - 2).wait()
-
+        scatter_x(c).wait_send()
+        scatter_y(c).wait_send()
         onward_x(c, 1 - x).wait_recv()
         onward_y(c, 1 - y).wait_recv()
         for q in range(4):
@@ -304,8 +290,7 @@
             grad = jnp.dot(hid_t[whole(c), :], og_v[:, cols], preferred_element_type=jnp.float32)
             kept = 0.42 * inner_v[slot, :, cols].astype(jnp.float32)
             kept = kept + 0.5 * gbf[q // 2, q % 2, whole(c)].astype(jnp.float32)
-            merged_v[slot, :, cols] = (kept - grad * factor[0:1, :]).astype(jnp.bfloat16)
-        merged_copy(c).start()
+            pseudo[q // 2, q % 2, whole(c)] = (kept - grad * factor[0:1, :]).astype(jnp.bfloat16)
 
         @pl.when(c + 2 < count)
         def _():
@@ -314,25 +299,37 @@
         return carry
 
     lax.fori_loop(0, count, merge_chunk, 0)
-    for c in range(max(count - 2, 0), count):
-        merged_copy(c).wait()
 
     def drain(c, carry):
-        scatter_x(c).wait_send()
-        scatter_y(c).wait_send()
         pass_y(c).wait_send()
         pass_x(c).wait_send()
         own_x(c, x).wait_send()
         own_y(c, y).wait_send()
         onward_x(c, x).wait_send()
         onward_y(c, y).wait_send()
-        glob_copy(c).wait()
-        mom_copy(c).wait()
         return carry
 
     lax.fori_loop(0, count, drain, 0)
     for step in range(1, shards):
         sum_copy(step).wait_send()
+
+
+def write_results(merged_v, glob_v, mom_v, merged_out, glob_out, mom_out, sem):
+    rows, quarter = glob_v.shape
+    copies = []
+    for q in range(4):
+        place = merged_out.at[:, pl.ds(quarter * q, quarter)]
+        copies.append(pltpu.make_async_copy(merged_v.at[q // 2, q % 2], place, sem.at[q]))
+    for index, (held, out) in enumerate(((glob_v, glob_out), (mom_v, mom_out))):
+        for part in range(2):
+            at = pl.ds(part * (rows // 2), rows // 2)
+            copies.append(
+                pltpu.make_async_copy(held.at[at], out.at[at], sem.at[4 + 2 * index + part])
+            )
+    for copy in copies:
+        copy.start()
+    for copy in copies:
+        copy.wait()
 
 
 def per_device_square(
@@ -347,17 +344,17 @@
     bf16, f32 = jnp.bfloat16, jnp.float32
     dma = pltpu.SemaphoreType.DMA
     any_spec = pl.BlockSpec(memory_space=pl.ANY)
+    vmem_spec = pl.BlockSpec(memory_space=pltpu.VMEM)
     merged, new_global, new_momentum = pl.pallas_call(
         functools.partial(fused_step, chunk, shards, tokens, rows * shards * width),
         out_shape=(
-            jax.ShapeDtypeStruct((rows, width), bf16),
-            jax.ShapeDtypeStruct((rows, quarter), f32),
-            jax.ShapeDtypeStruct((rows, quarter), f32),
+            pltpu.VMEM((2, 2, rows, quarter), bf16),
+            pltpu.VMEM((rows, quarter), f32),
+            pltpu.VMEM((rows, quarter), f32),
         ),
         in_specs=[any_spec] * 8,
-        out_specs=(any_spec,) * 3,
+        out_specs=(vmem_spec,) * 3,
         scratch_shapes=[
-            pltpu.VMEM((2, 2, rows, quarter), bf16),
             pltpu.VMEM((2, rows // 2, quarter), bf16),
             pltpu.VMEM((2, rows // 2, quarter), bf16),
             pltpu.VMEM((rows // 2, quarter), bf16),
@@ -365,15 +362,12 @@
             pltpu.VMEM((rows // 2, quarter), bf16),
             pltpu.VMEM((rows // 2, quarter), bf16),
             pltpu.VMEM((2, 2, rows, quarter), bf16),
-            pltpu.VMEM((rows, quarter), f32),
-            pltpu.VMEM((rows, quarter), f32),
             pltpu.VMEM((SLOTS, chunk, width // 2), jnp.int32),
-            pltpu.VMEM(code_scales.shape[1:], f32),
+            pltpu.VMEM((code_scales.shape[2], rows), f32),
             pltpu.VMEM((tokens, rows), bf16),
             pltpu.VMEM((tokens, rows), bf16),
             pltpu.VMEM((tokens, width), bf16),
             pltpu.VMEM((rows, tokens), bf16),
-            pltpu.VMEM((2, chunk, width), bf16),
             pltpu.VMEM((2, chunk, width), bf16),
             pltpu.VMEM((256, 256), bf16),
             pltpu.VMEM((8, quarter), f32),
@@ -386,19 +380,32 @@
             dma((SLOTS,)),
             dma((6,)),
             dma((2,)),
-            dma((2,)),
-            dma((2, count)),
         ],
         compiler_params=pltpu.CompilerParams(
-            collective_id=0, has_side_effects=True, vmem_limit_bytes=60 * 1024 * 1024
+            collective_id=0, has_side_effects=True, vmem_limit_bytes=40 * 1024 * 1024
         ),
         cost_estimate=pl.CostEstimate(
             flops=4 * tokens * rows * width, bytes_accessed=22 * rows * width, transcendentals=0
         ),
     )(
         gate_pre, up_pre, out_grad, inner_params[0], global_params, outer_momentum,
-        pair_codes[0], code_scales[0],
+        pair_codes[0], code_scales[0].T,
     )
+    merged, new_global, new_momentum = pl.pallas_call(
+        write_results,
+        out_shape=(
+            jax.ShapeDtypeStruct((rows, width), bf16),
+            jax.ShapeDtypeStruct((rows, quarter), f32),
+            jax.ShapeDtypeStruct((rows, quarter), f32),
+        ),
+        in_specs=[vmem_spec] * 3,
+        out_specs=(any_spec,) * 3,
+        scratch_shapes=[dma((8,))],
+        compiler_params=pltpu.CompilerParams(vmem_limit_bytes=4 * 1024 * 1024),
+        cost_estimate=pl.CostEstimate(
+            flops=0, bytes_accessed=4 * rows * width, transcendentals=0
+        ),
+    )(merged, new_global, new_momentum)
     return (merged[None], new_global, new_momentum)
 
 

time: 182 us -> 170 us (0.934)
  local copies, waits for them, and re-layouts: 17.5 us -> 0 us
  Pallas kernels: 164 us -> 169 us
    unnamed x6 -> x0, local copies, waits for them, and re-layouts: 17.5 us -> none
    pallas_call x0 -> x1, Pallas kernels: none -> 6.58 us  [per_device_square(): pl.pallas_call(write_results, out_shape=(jax.ShapeDtypeStruct((rows, widt...]
where the time goes in v2:
time: 170 us
  Pallas kernels  169 us (99%)
    pallas_call x1, Pallas kernels, per_device_square(): pl.pallas_call(functools.partial(fused_step, chunk, shards, tokens, rows...  163 us
    pallas_call x1, Pallas kernels, per_device_square(): pl.pallas_call(write_results, out_shape=(jax.ShapeDtypeStruct((rows, widt...  6.58 us

profile of v2, /device:TPU:0, one launch (start us, length us, event | category | flops | bytes accessed | tf_op | source)
XLA Modules:
  0.0 170.0 jit_solution(7553648333072921425)
XLA Ops:
  0.6 162.8 %shard_map.103 = (bf16[2,2,1536,768]{3,2,1,0:T(8,128)(2,1)S(1)}, f32[1536,768]{1,0:T(8,128)S(1)}, f32[1536,768]{1,0:T(8,128)S(1)}) custom-call(bf16[512,1536]{1,0:T(8,128)(2,1)} %gate.1, bf16[512,1536]{1,0:T(8,128)(2,1)} %up.1, bf16[512,3072]{1,0:T(8,128)(2,1)} %og.1, bf16[1536,3072]{1,0:T(8,128)(2,1)} %bitcast.6, f32[1536,768]{1,0:T(8,128)} %glob.1, ...), custom_call_target="tpu_custom_call" | custom-call | flops 9663676416 | bytes 103809024 | tf_op jit(solution)/shard_map/pallas_call | solution.py:348
  163.4 6.6 %shard_map.104 = (bf16[1536,3072]{1,0:T(8,128)(2,1)}, f32[1536,768]{1,0:T(8,128)}, f32[1536,768]{1,0:T(8,128)}) custom-call(bf16[2,2,1536,768]{3,2,1,0:T(8,128)(2,1)S(1)} %get-tuple-element.9.merged_v, f32[1536,768]{1,0:T(8,128)S(1)} %get-tuple-element.10.glob_v, f32[1536,768]{1,0:T(8,128)S(1)} %get-tuple-element.11.mom_v), custom_call_target="tpu_custom_call" | custom-call | bytes 18874368 | tf_op jit(solution)/shard_map/pallas_call | solution.py:394

commit v3 on v2

--- a/solution.py
+++ b/solution.py
@@ -57,6 +57,7 @@
 
 
 SLOTS = 4
+LAG = 2
 MESH = pl.DeviceIdType.MESH
 
 
@@ -138,6 +139,17 @@
     def inner_copy(c):
         return pltpu.make_async_copy(inner.at[whole(c)], inner_v.at[c % 2], inner_sem.at[c % 2])
 
+    scale_load = pltpu.make_async_copy(scales, scale_v, load_sem.at[0])
+    gate_load = pltpu.make_async_copy(gate, gate_v, load_sem.at[1])
+    up_load = pltpu.make_async_copy(up, up_v, load_sem.at[2])
+    og_load = pltpu.make_async_copy(og, og_v, load_sem.at[3])
+    glob_load = pltpu.make_async_copy(glob, glob_v, load_sem.at[4])
+    mom_load = pltpu.make_async_copy(mom, mom_v, load_sem.at[5])
+    code_copy(0).start()
+    scale_load.start()
+    for c in range(1, min(SLOTS, count)):
+        code_copy(c).start()
+
     barrier = pltpu.get_barrier_semaphore()
     for peer in (x_peer, y_peer):
         pl.semaphore_signal(barrier, inc=1, device_id=(peer, shard), device_id_type=MESH)
@@ -146,20 +158,6 @@
             barrier, inc=1, device_id=(rep, (shard + step) % shards), device_id_type=MESH
         )
 
-    scale_load = pltpu.make_async_copy(scales, scale_v, load_sem.at[0])
-    gate_load = pltpu.make_async_copy(gate, gate_v, load_sem.at[1])
-    up_load = pltpu.make_async_copy(up, up_v, load_sem.at[2])
-    og_load = pltpu.make_async_copy(og, og_v, load_sem.at[3])
-    glob_load = pltpu.make_async_copy(glob, glob_v, load_sem.at[4])
-    mom_load = pltpu.make_async_copy(mom, mom_v, load_sem.at[5])
-    scale_load.start()
-    for c in range(min(SLOTS, count)):
-        code_copy(c).start()
-    for load in (gate_load, up_load, og_load, glob_load, mom_load):
-        load.start()
-    for c in range(min(2, count)):
-        inner_copy(c).start()
-
     k = lax.broadcasted_iota(jnp.int32, (256, 256), 0)
     n = lax.broadcasted_iota(jnp.int32, (256, 256), 1)
     j, odd = n >> 1, n & 1
@@ -168,10 +166,7 @@
     spread[...] = (from_word + from_upper).astype(jnp.bfloat16)
     squares[...] = jnp.zeros_like(squares)
 
-    scale_load.wait()
-    pl.semaphore_wait(barrier, shards + 1)
-
-    def unpack_chunk(c, carry):
+    def unpack_chunk(c):
         code_copy(c).wait()
         block_scale = scale_v[:, whole(c)].T
         slot = c % SLOTS
@@ -191,23 +186,14 @@
                 value = centered[:, 128 * part : 128 * part + 128]
                 value = value * block_scale[:, 2 * b + part : 2 * b + part + 1]
                 pseudo[q // 2, q % 2, whole(c), at : at + 128] = value.astype(jnp.bfloat16)
-        scatter_x(c).start()
-        scatter_y(c).start()
 
         @pl.when(c + SLOTS < count)
         def _():
             code_copy(c + SLOTS).start()
 
-        return carry
-
-    lax.fori_loop(0, count, unpack_chunk, 0)
-
-    gate_load.wait()
-    up_load.wait()
-    og_load.wait()
-
-    def square_chunk(c, carry):
-        cols = whole(c)
+    def square_chunk(c):
+        wide = 2 * chunk
+        cols = pl.ds(pl.multiple_of(c * wide, wide), wide)
         g = gate_v[:, cols].astype(jnp.float32)
         h = g * jax.nn.sigmoid(g) * up_v[:, cols].astype(jnp.float32)
         hid_t[cols, :] = h.T.astype(jnp.bfloat16)
@@ -216,15 +202,14 @@
                 hid_t[cols, :], og_v[:, quarter * q : quarter * (q + 1)],
                 preferred_element_type=jnp.float32,
             ) * (1.0 / tok_total)
-            squares[...] += jnp.sum((grad * grad).reshape(chunk // 8, 8, quarter), axis=0)
-        return carry
-
-    lax.fori_loop(0, count, square_chunk, 0)
-    sums[0] = jnp.full((8, 128), jnp.sum(squares[...]), jnp.float32)
-    for step in range(1, shards):
-        sum_copy(step).start()
-
-    def pass_chunk(c, carry):
+            squares[...] += jnp.sum((grad * grad).reshape(wide // 8, 8, quarter), axis=0)
+
+    def send_sums():
+        sums[0] = jnp.full((8, 128), jnp.sum(squares[...]), jnp.float32)
+        for step in range(1, shards):
+            sum_copy(step).start()
+
+    def pass_chunk(c):
         scatter_x(c).wait_recv()
         mine = pseudo[1 - y, x, first(c)].astype(jnp.float32)
         sa[packed(c)] = (mine + ra[1 - y, packed(c)].astype(jnp.float32)).astype(jnp.bfloat16)
@@ -233,11 +218,6 @@
         mine = pseudo[y, 1 - x, second(c)].astype(jnp.float32)
         sb[packed(c)] = (mine + rb[1 - x, packed(c)].astype(jnp.float32)).astype(jnp.bfloat16)
         pass_x(c).start()
-        return carry
-
-    lax.fori_loop(0, count, pass_chunk, 0)
-    glob_load.wait()
-    mom_load.wait()
 
     def outer_rows(at, total):
         new_momentum, new_global = outer_update(total * 0.25, mom_v[at], glob_v[at])
@@ -245,7 +225,7 @@
         glob_v[at] = new_global
         gbf[y, x, at] = new_global.astype(jnp.bfloat16)
 
-    def outer_chunk(c, carry):
+    def outer_chunk(c):
         f32 = jnp.float32
         pass_y(c).wait_recv()
         at, near = first(c), packed(c)
@@ -255,29 +235,24 @@
         outer_rows(at, pseudo[y, x, at].astype(f32) + rb[x, near].astype(f32) + r2b[near].astype(f32))
         own_x(c, x).start()
         own_y(c, y).start()
-        return carry
-
-    lax.fori_loop(0, count, outer_chunk, 0)
-
-    for step in range(1, shards):
-        sum_copy(step).wait_recv()
-    total = sums[0]
-    for step in range(1, shards):
-        total = total + sums[step]
-    root_mean = jnp.sqrt(total / all_entries + 1e-06)
-    scale = jnp.minimum(1.0, 0.02 / root_mean) * (0.4 / tok_total)
-    factor[...] = jnp.concatenate([scale] * (quarter // 128), axis=1)
-
-    def onward_chunk(c, carry):
+
+    def find_factor():
+        for step in range(1, shards):
+            sum_copy(step).wait_recv()
+        total = sums[0]
+        for step in range(1, shards):
+            total = total + sums[step]
+        root_mean = jnp.sqrt(total / all_entries + 1e-06)
+        scale = jnp.minimum(1.0, 0.02 / root_mean) * (0.4 / tok_total)
+        factor[...] = jnp.concatenate([scale] * (quarter // 128), axis=1)
+
+    def onward_chunk(c):
         own_y(c, 1 - y).wait_recv()
         onward_x(c, x).start()
         own_x(c, 1 - x).wait_recv()
         onward_y(c, y).start()
-        return carry
-
-    lax.fori_loop(0, count, onward_chunk, 0)
-
-    def merge_chunk(c, carry):
+
+    def merge_chunk(c):
         slot = c % 2
         inner_copy(c).wait()
 
@@ -296,9 +271,68 @@
         def _():
             inner_copy(c + 2).start()
 
+    scale_load.wait()
+    unpack_chunk(0)
+    pl.semaphore_wait(barrier, shards + 1)
+    for load in (gate_load, up_load, og_load, glob_load, mom_load):
+        load.start()
+    for c in range(min(2, count)):
+        inner_copy(c).start()
+
+    merge_lag = max(4 * LAG, LAG + count // 2)
+
+    def step(s, carry):
+        @pl.when(s < count)
+        def _():
+            scatter_x(s).start()
+            scatter_y(s).start()
+
+        @pl.when(s + 1 < count)
+        def _():
+            unpack_chunk(s + 1)
+
+        @pl.when((s >= LAG) & (s < count + LAG))
+        def _():
+            pass_chunk(s - LAG)
+
+        @pl.when(s == 2 * LAG)
+        def _():
+            glob_load.wait()
+            mom_load.wait()
+
+        @pl.when((s >= 2 * LAG) & (s < count + 2 * LAG))
+        def _():
+            outer_chunk(s - 2 * LAG)
+
+        @pl.when((s >= 3 * LAG) & (s < count + 3 * LAG))
+        def _():
+            onward_chunk(s - 3 * LAG)
+
+        @pl.when(s == LAG)
+        def _():
+            gate_load.wait()
+            up_load.wait()
+            og_load.wait()
+
+        @pl.when((s >= LAG) & (s < LAG + count // 2))
+        def _():
+            square_chunk(s - LAG)
+
+        @pl.when(s == LAG + count // 2 - 1)
+        def _():
+            send_sums()
+
+        @pl.when(s == merge_lag)
+        def _():
+            find_factor()
+
+        @pl.when(s >= merge_lag)
+        def _():
+            merge_chunk(s - merge_lag)
+
         return carry
 
-    lax.fori_loop(0, count, merge_chunk, 0)
+    lax.fori_loop(0, count + merge_lag, step, 0)
 
     def drain(c, carry):
         pass_y(c).wait_send()
@@ -412,7 +446,7 @@
 def per_device(*arrays):
     rows, width = arrays[0].shape[1], arrays[2].shape[1]
     square = lax.axis_size("rep") == 4 and lax.axis_size("fsdp") > 1
-    if square and rows % 128 == 0 and width % 1024 == 0 and width // arrays[7].shape[2] == 128:
+    if square and rows % 256 == 0 and width % 1024 == 0 and width // arrays[7].shape[2] == 128:
         return per_device_square(*arrays)
     return per_device_any(*arrays)
 

time: 170 us -> 169 us (level)
  no operation moved by 1% of the time
where the time goes in v3:
time: 169 us
  Pallas kernels  169 us (100%)
    pallas_call x1, Pallas kernels, per_device_square(): pl.pallas_call(functools.partial(fused_step, chunk, shards, tokens, rows...  162 us
    pallas_call x1, Pallas kernels, per_device_square(): pl.pallas_call(write_results, out_shape=(jax.ShapeDtypeStruct((rows, widt...  6.58 us

profile of v3, /device:TPU:0, one launch (start us, length us, event | category | flops | bytes accessed | tf_op | source)
XLA Modules:
  0.0 169.3 jit_solution(2070823659665596468)
XLA Ops:
  0.6 162.1 %shard_map.103 = (bf16[2,2,1536,768]{3,2,1,0:T(8,128)(2,1)S(1)}, f32[1536,768]{1,0:T(8,128)S(1)}, f32[1536,768]{1,0:T(8,128)S(1)}) custom-call(bf16[512,1536]{1,0:T(8,128)(2,1)} %gate.1, bf16[512,1536]{1,0:T(8,128)(2,1)} %up.1, bf16[512,3072]{1,0:T(8,128)(2,1)} %og.1, bf16[1536,3072]{1,0:T(8,128)(2,1)} %bitcast.6, f32[1536,768]{1,0:T(8,128)} %glob.1, ...), custom_call_target="tpu_custom_call" | custom-call | flops 9663676416 | bytes 103809024 | tf_op jit(solution)/shard_map/pallas_call | solution.py:382
  162.7 6.6 %shard_map.104 = (bf16[1536,3072]{1,0:T(8,128)(2,1)}, f32[1536,768]{1,0:T(8,128)}, f32[1536,768]{1,0:T(8,128)}) custom-call(bf16[2,2,1536,768]{3,2,1,0:T(8,128)(2,1)S(1)} %get-tuple-element.9.merged_v, f32[1536,768]{1,0:T(8,128)S(1)} %get-tuple-element.10.glob_v, f32[1536,768]{1,0:T(8,128)S(1)} %get-tuple-element.11.mom_v), custom_call_target="tpu_custom_call" | custom-call | bytes 18874368 | tf_op jit(solution)/shard_map/pallas_call | solution.py:428

commit v4 on v3

--- a/solution.py
+++ b/solution.py
@@ -57,7 +57,8 @@
 
 
 SLOTS = 4
-LAG = 2
+PASS_LAG, OUTER_LAG, ONWARD_LAG, MERGE_LAG = 4, 7, 10, 13
+WIDE = 256
 MESH = pl.DeviceIdType.MESH
 
 
@@ -66,7 +67,7 @@
     gate, up, og, inner, glob, mom, codes, scales,
     pseudo, glob_v, mom_v,
     ra, rb, sa, sb, r2a, r2b, gbf, code_v, scale_v,
-    gate_v, up_v, og_v, hid_t, inner_v, spread, squares, sums, factor,
+    gate_v, up_v, og_v, hid_t, inner_v, base, scale_t, spread, squares, sums, factor,
     send_sem, recv_sem, sum_send, sum_recv, code_sem, load_sem, inner_sem,
 ):
     rows = glob_v.shape[0]
@@ -168,7 +169,14 @@
 
     def unpack_chunk(c):
         code_copy(c).wait()
-        block_scale = scale_v[:, whole(c)].T
+        share = 128 // chunk
+
+        @pl.when(c % share == 0)
+        def _():
+            lanes = pl.ds(pl.multiple_of(c // share * 128, 128), 128)
+            scale_t[...] = scale_v[:, lanes].T
+
+        block_scale = scale_t[pl.ds(pl.multiple_of(c % share * chunk, chunk), chunk), :]
         slot = c % SLOTS
         for b in range(code_v.shape[2] // 128):
             word = code_v[slot, :, 128 * b : 128 * b + 128]
@@ -192,8 +200,7 @@
             code_copy(c + SLOTS).start()
 
     def square_chunk(c):
-        wide = 2 * chunk
-        cols = pl.ds(pl.multiple_of(c * wide, wide), wide)
+        cols = pl.ds(pl.multiple_of(c * WIDE, WIDE), WIDE)
         g = gate_v[:, cols].astype(jnp.float32)
         h = g * jax.nn.sigmoid(g) * up_v[:, cols].astype(jnp.float32)
         hid_t[cols, :] = h.T.astype(jnp.bfloat16)
@@ -202,7 +209,7 @@
                 hid_t[cols, :], og_v[:, quarter * q : quarter * (q + 1)],
                 preferred_element_type=jnp.float32,
             ) * (1.0 / tok_total)
-            squares[...] += jnp.sum((grad * grad).reshape(wide // 8, 8, quarter), axis=0)
+            squares[...] += jnp.sum((grad * grad).reshape(WIDE // 8, 8, quarter), axis=0)
 
     def send_sums():
         sums[0] = jnp.full((8, 128), jnp.sum(squares[...]), jnp.float32)
@@ -256,20 +263,24 @@
         slot = c % 2
         inner_copy(c).wait()
 
+        for q in range(4):
+            cols = slice(quarter * q, quarter * (q + 1))
+            grad = jnp.dot(hid_t[whole(c), :], og_v[:, cols], preferred_element_type=jnp.float32)
+            kept = 0.42 * inner_v[slot, :, cols].astype(jnp.float32)
+            base[:, cols] = kept - grad * factor[0:1, :]
+
+        @pl.when(c + 2 < count)
+        def _():
+            inner_copy(c + 2).start()
+
         scatter_x(c).wait_send()
         scatter_y(c).wait_send()
         onward_x(c, 1 - x).wait_recv()
         onward_y(c, 1 - y).wait_recv()
         for q in range(4):
-            cols = slice(quarter * q, quarter * (q + 1))
-            grad = jnp.dot(hid_t[whole(c), :], og_v[:, cols], preferred_element_type=jnp.float32)
-            kept = 0.42 * inner_v[slot, :, cols].astype(jnp.float32)
-            kept = kept + 0.5 * gbf[q // 2, q % 2, whole(c)].astype(jnp.float32)
-            pseudo[q // 2, q % 2, whole(c)] = (kept - grad * factor[0:1, :]).astype(jnp.bfloat16)
-
-        @pl.when(c + 2 < count)
-        def _():
-            inner_copy(c + 2).start()
+            arrived = gbf[q // 2, q % 2, whole(c)].astype(jnp.float32)
+            kept = base[:, quarter * q : quarter * (q + 1)] + 0.5 * arrived
+            pseudo[q // 2, q % 2, whole(c)] = kept.astype(jnp.bfloat16)
 
     scale_load.wait()
     unpack_chunk(0)
@@ -279,7 +290,7 @@
     for c in range(min(2, count)):
         inner_copy(c).start()
 
-    merge_lag = max(4 * LAG, LAG + count // 2)
+    merge_lag = max(MERGE_LAG, PASS_LAG + rows // WIDE)
 
     def step(s, carry):
         @pl.when(s < count)
@@ -291,34 +302,34 @@
         def _():
             unpack_chunk(s + 1)
 
-        @pl.when((s >= LAG) & (s < count + LAG))
-        def _():
-            pass_chunk(s - LAG)
-
-        @pl.when(s == 2 * LAG)
+        @pl.when((s >= PASS_LAG) & (s < count + PASS_LAG))
+        def _():
+            pass_chunk(s - PASS_LAG)
+
+        @pl.when(s == OUTER_LAG)
         def _():
             glob_load.wait()
             mom_load.wait()
 
-        @pl.when((s >= 2 * LAG) & (s < count + 2 * LAG))
-        def _():
-            outer_chunk(s - 2 * LAG)
-
-        @pl.when((s >= 3 * LAG) & (s < count + 3 * LAG))
-        def _():
-            onward_chunk(s - 3 * LAG)
-
-        @pl.when(s == LAG)
+        @pl.when((s >= OUTER_LAG) & (s < count + OUTER_LAG))
+        def _():
+            outer_chunk(s - OUTER_LAG)
+
+        @pl.when((s >= ONWARD_LAG) & (s < count + ONWARD_LAG))
+        def _():
+            onward_chunk(s - ONWARD_LAG)
+
+        @pl.when(s == PASS_LAG)
         def _():
             gate_load.wait()
             up_load.wait()
             og_load.wait()
 
-        @pl.when((s >= LAG) & (s < LAG + count // 2))
-        def _():
-            square_chunk(s - LAG)
-
-        @pl.when(s == LAG + count // 2 - 1)
+        @pl.when((s >= PASS_LAG) & (s < PASS_LAG + rows // WIDE))
+        def _():
+            square_chunk(s - PASS_LAG)
+
+        @pl.when(s == PASS_LAG + rows // WIDE - 1)
         def _():
             send_sums()
 
@@ -352,14 +363,16 @@
     rows, quarter = glob_v.shape
     copies = []
     for q in range(4):
-        place = merged_out.at[:, pl.ds(quarter * q, quarter)]
-        copies.append(pltpu.make_async_copy(merged_v.at[q // 2, q % 2], place, sem.at[q]))
-    for index, (held, out) in enumerate(((glob_v, glob_out), (mom_v, mom_out))):
         for part in range(2):
             at = pl.ds(part * (rows // 2), rows // 2)
+            place = merged_out.at[at, pl.ds(quarter * q, quarter)]
             copies.append(
-                pltpu.make_async_copy(held.at[at], out.at[at], sem.at[4 + 2 * index + part])
+                pltpu.make_async_copy(merged_v.at[q // 2, q % 2, at], place, sem.at[len(copies)])
             )
+    for held, out in ((glob_v, glob_out), (mom_v, mom_out)):
+        for part in range(4):
+            at = pl.ds(part * (rows // 4), rows // 4)
+            copies.append(pltpu.make_async_copy(held.at[at], out.at[at], sem.at[len(copies)]))
     for copy in copies:
         copy.start()
     for copy in copies:
@@ -373,7 +386,7 @@
     tokens, rows = gate_pre.shape
     width = out_grad.shape[1]
     quarter = width // 4
-    chunk = 128
+    chunk = 64
     count = rows // chunk
     bf16, f32 = jnp.bfloat16, jnp.float32
     dma = pltpu.SemaphoreType.DMA
@@ -403,6 +416,8 @@
             pltpu.VMEM((tokens, width), bf16),
             pltpu.VMEM((rows, tokens), bf16),
             pltpu.VMEM((2, chunk, width), bf16),
+            pltpu.VMEM((chunk, width), f32),
+            pltpu.VMEM((128, code_scales.shape[2]), f32),
             pltpu.VMEM((256, 256), bf16),
             pltpu.VMEM((8, quarter), f32),
             pltpu.VMEM((shards, 8, 128), f32),
@@ -434,7 +449,7 @@
         ),
         in_specs=[vmem_spec] * 3,
         out_specs=(any_spec,) * 3,
-        scratch_shapes=[dma((8,))],
+        scratch_shapes=[dma((16,))],
         compiler_params=pltpu.CompilerParams(vmem_limit_bytes=4 * 1024 * 1024),
         cost_estimate=pl.CostEstimate(
             flops=0, bytes_accessed=4 * rows * width, transcendentals=0
@@ -446,7 +461,7 @@
 def per_device(*arrays):
     rows, width = arrays[0].shape[1], arrays[2].shape[1]
     square = lax.axis_size("rep") == 4 and lax.axis_size("fsdp") > 1
-    if square and rows % 256 == 0 and width % 1024 == 0 and width // arrays[7].shape[2] == 128:
+    if square and rows % WIDE == 0 and width % 1024 == 0 and width // arrays[7].shape[2] == 128:
         return per_device_square(*arrays)
     return per_device_any(*arrays)
 

time: 169 us -> 171 us (1.012)
  no operation moved by 1% of the time
where the time goes in v4:
time: 171 us
  Pallas kernels  170 us (99%)
    pallas_call x1, Pallas kernels, per_device_square(): pl.pallas_call(functools.partial(fused_step, chunk, shards, tokens, rows...  164 us
    pallas_call x1, Pallas kernels, per_device_square(): pl.pallas_call(write_results, out_shape=(jax.ShapeDtypeStruct((rows, widt...  6.61 us

profile of v4, /device:TPU:0, one launch (start us, length us, event | category | flops | bytes accessed | tf_op | source)
XLA Modules:
  0.0 170.9 jit_solution(8386155841951275578)
XLA Ops:
  0.6 163.7 %shard_map.103 = (bf16[2,2,1536,768]{3,2,1,0:T(8,128)(2,1)S(1)}, f32[1536,768]{1,0:T(8,128)S(1)}, f32[1536,768]{1,0:T(8,128)S(1)}) custom-call(bf16[512,1536]{1,0:T(8,128)(2,1)} %gate.1, bf16[512,1536]{1,0:T(8,128)(2,1)} %up.1, bf16[512,3072]{1,0:T(8,128)(2,1)} %og.1, bf16[1536,3072]{1,0:T(8,128)(2,1)} %bitcast.6, f32[1536,768]{1,0:T(8,128)} %glob.1, ...), custom_call_target="tpu_custom_call" | custom-call | flops 9663676416 | bytes 103809024 | tf_op jit(solution)/shard_map/pallas_call | solution.py:395
  164.3 6.6 %shard_map.104 = (bf16[1536,3072]{1,0:T(8,128)(2,1)}, f32[1536,768]{1,0:T(8,128)}, f32[1536,768]{1,0:T(8,128)}) custom-call(bf16[2,2,1536,768]{3,2,1,0:T(8,128)(2,1)S(1)} %get-tuple-element.9.merged_v, f32[1536,768]{1,0:T(8,128)S(1)} %get-tuple-element.10.glob_v, f32[1536,768]{1,0:T(8,128)S(1)} %get-tuple-element.11.mom_v), custom_call_target="tpu_custom_call" | custom-call | bytes 18874368 | tf_op jit(solution)/shard_map/pallas_call | solution.py:443

commit v5 on v3

--- a/solution.py
+++ b/solution.py
@@ -66,8 +66,8 @@
     gate, up, og, inner, glob, mom, codes, scales,
     pseudo, glob_v, mom_v,
     ra, rb, sa, sb, r2a, r2b, gbf, code_v, scale_v,
-    gate_v, up_v, og_v, hid_t, inner_v, spread, squares, sums, factor,
-    send_sem, recv_sem, sum_send, sum_recv, code_sem, load_sem, inner_sem,
+    gate_v, up_v, og_v, hid_t, inner_v, base, spread, squares, sums, factor,
+    send_sem, recv_sem, sum_send, sum_recv, code_sem, load_sem, inner_sem, ready, opened,
 ):
     rows = glob_v.shape[0]
     quarter = glob_v.shape[1]
@@ -151,12 +151,49 @@
         code_copy(c).start()
 
     barrier = pltpu.get_barrier_semaphore()
-    for peer in (x_peer, y_peer):
-        pl.semaphore_signal(barrier, inc=1, device_id=(peer, shard), device_id_type=MESH)
-    for step in range(1, shards):
-        pl.semaphore_signal(
-            barrier, inc=1, device_id=(rep, (shard + step) % shards), device_id_type=MESH
-        )
+
+    def signal(semaphore, peer, at_shard):
+        pl.semaphore_signal(semaphore, inc=1, device_id=(peer, at_shard), device_id_type=MESH)
+
+    @pl.when(rep == 0)
+    def _():
+        for peer in (1, 2, 3):
+            signal(barrier, peer, shard)
+
+    @pl.when(rep == 3)
+    def _():
+        for peer in (1, 2):
+            signal(barrier, peer, shard)
+
+    def enter():
+        @pl.when((rep == 1) | (rep == 2))
+        def _():
+            pl.semaphore_wait(barrier, 2)
+            for peer in (0, 3):
+                signal(ready, peer, shard)
+
+        @pl.when(rep == 3)
+        def _():
+            pl.semaphore_wait(barrier, 1)
+            signal(ready, 0, shard)
+            pl.semaphore_wait(ready, 2)
+
+        @pl.when(rep == 0)
+        def _():
+            pl.semaphore_wait(ready, 3)
+            for step in range(1, shards):
+                signal(barrier, 0, (shard + step) % shards)
+
+    def enter_shards():
+        @pl.when(rep == 0)
+        def _():
+            pl.semaphore_wait(barrier, shards - 1)
+            for peer in (1, 2, 3):
+                signal(opened, peer, shard)
+
+        @pl.when(rep > 0)
+        def _():
+            pl.semaphore_wait(opened, 1)
 
     k = lax.broadcasted_iota(jnp.int32, (256, 256), 0)
     n = lax.broadcasted_iota(jnp.int32, (256, 256), 1)
@@ -205,6 +242,7 @@
             squares[...] += jnp.sum((grad * grad).reshape(wide // 8, 8, quarter), axis=0)
 
     def send_sums():
+        enter_shards()
         sums[0] = jnp.full((8, 128), jnp.sum(squares[...]), jnp.float32)
         for step in range(1, shards):
             sum_copy(step).start()
@@ -256,24 +294,28 @@
         slot = c % 2
         inner_copy(c).wait()
 
+        for q in range(4):
+            cols = slice(quarter * q, quarter * (q + 1))
+            grad = jnp.dot(hid_t[whole(c), :], og_v[:, cols], preferred_element_type=jnp.float32)
+            kept = 0.42 * inner_v[slot, :, cols].astype(jnp.float32)
+            base[:, cols] = kept - grad * factor[0:1, :]
+
+        @pl.when(c + 2 < count)
+        def _():
+            inner_copy(c + 2).start()
+
         scatter_x(c).wait_send()
         scatter_y(c).wait_send()
         onward_x(c, 1 - x).wait_recv()
         onward_y(c, 1 - y).wait_recv()
         for q in range(4):
-            cols = slice(quarter * q, quarter * (q + 1))
-            grad = jnp.dot(hid_t[whole(c), :], og_v[:, cols], preferred_element_type=jnp.float32)
-            kept = 0.42 * inner_v[slot, :, cols].astype(jnp.float32)
-            kept = kept + 0.5 * gbf[q // 2, q % 2, whole(c)].astype(jnp.float32)
-            pseudo[q // 2, q % 2, whole(c)] = (kept - grad * factor[0:1, :]).astype(jnp.bfloat16)
-
-        @pl.when(c + 2 < count)
-        def _():
-            inner_copy(c + 2).start()
+            arrived = gbf[q // 2, q % 2, whole(c)].astype(jnp.float32)
+            kept = base[:, quarter * q : quarter * (q + 1)] + 0.5 * arrived
+            pseudo[q // 2, q % 2, whole(c)] = kept.astype(jnp.bfloat16)
 
     scale_load.wait()
     unpack_chunk(0)
-    pl.semaphore_wait(barrier, shards + 1)
+    enter()
     for load in (gate_load, up_load, og_load, glob_load, mom_load):
         load.start()
     for c in range(min(2, count)):
@@ -403,6 +445,7 @@
             pltpu.VMEM((tokens, width), bf16),
             pltpu.VMEM((rows, tokens), bf16),
             pltpu.VMEM((2, chunk, width), bf16),
+            pltpu.VMEM((chunk, width), f32),
             pltpu.VMEM((256, 256), bf16),
             pltpu.VMEM((8, quarter), f32),
             pltpu.VMEM((shards, 8, 128), f32),
@@ -414,6 +457,8 @@
             dma((SLOTS,)),
             dma((6,)),
             dma((2,)),
+            pltpu.SemaphoreType.REGULAR,
+            pltpu.SemaphoreType.REGULAR,
         ],
         compiler_params=pltpu.CompilerParams(
             collective_id=0, has_side_effects=True, vmem_limit_bytes=40 * 1024 * 1024

time: 169 us -> 167 us (0.988)
  Pallas kernels: 169 us -> 167 us
    pallas_call x1, Pallas kernels: 162 us -> 160 us  [per_device_square(): pl.pallas_call(functools.partial(fused_step, chunk, shards, tokens, rows...]
where the time goes in v5:
time: 167 us
  Pallas kernels  167 us (100%)
    pallas_call x1, Pallas kernels, per_device_square(): pl.pallas_call(functools.partial(fused_step, chunk, shards, tokens, rows...  160 us
    pallas_call x1, Pallas kernels, per_device_square(): pl.pallas_call(write_results, out_shape=(jax.ShapeDtypeStruct((rows, widt...  6.58 us

profile of v5, /device:TPU:0, one launch (start us, length us, event | category | flops | bytes accessed | tf_op | source)
XLA Modules:
  0.0 167.3 jit_solution(2132222288416427765)
XLA Ops:
  0.6 160.0 %shard_map.103 = (bf16[2,2,1536,768]{3,2,1,0:T(8,128)(2,1)S(1)}, f32[1536,768]{1,0:T(8,128)S(1)}, f32[1536,768]{1,0:T(8,128)S(1)}) custom-call(bf16[512,1536]{1,0:T(8,128)(2,1)} %gate.1, bf16[512,1536]{1,0:T(8,128)(2,1)} %up.1, bf16[512,3072]{1,0:T(8,128)(2,1)} %og.1, bf16[1536,3072]{1,0:T(8,128)(2,1)} %bitcast.6, f32[1536,768]{1,0:T(8,128)} %glob.1, ...), custom_call_target="tpu_custom_call" | custom-call | flops 9663676416 | bytes 103809024 | tf_op jit(solution)/shard_map/pallas_call | solution.py:424
  160.7 6.6 %shard_map.104 = (bf16[1536,3072]{1,0:T(8,128)(2,1)}, f32[1536,768]{1,0:T(8,128)}, f32[1536,768]{1,0:T(8,128)}) custom-call(bf16[2,2,1536,768]{3,2,1,0:T(8,128)(2,1)S(1)} %get-tuple-element.9.merged_v, f32[1536,768]{1,0:T(8,128)S(1)} %get-tuple-element.10.glob_v, f32[1536,768]{1,0:T(8,128)S(1)} %get-tuple-element.11.mom_v), custom_call_target="tpu_custom_call" | custom-call | bytes 18874368 | tf_op jit(solution)/shard_map/pallas_call | solution.py:473

commit v6 on v5

--- a/solution.py
+++ b/solution.py
@@ -313,9 +313,9 @@
             kept = base[:, quarter * q : quarter * (q + 1)] + 0.5 * arrived
             pseudo[q // 2, q % 2, whole(c)] = kept.astype(jnp.bfloat16)
 
+    enter()
     scale_load.wait()
     unpack_chunk(0)
-    enter()
     for load in (gate_load, up_load, og_load, glob_load, mom_load):
         load.start()
     for c in range(min(2, count)):

time: 167 us -> 167 us (level)
  no operation moved by 1% of the time
where the time goes in v6:
time: 167 us
  Pallas kernels  167 us (100%)
    pallas_call x1, Pallas kernels, per_device_square(): pl.pallas_call(functools.partial(fused_step, chunk, shards, tokens, rows...  160 us
    pallas_call x1, Pallas kernels, per_device_square(): pl.pallas_call(write_results, out_shape=(jax.ShapeDtypeStruct((rows, widt...  6.58 us

profile of v6, /device:TPU:0, one launch (start us, length us, event | category | flops | bytes accessed | tf_op | source)
XLA Modules:
  0.0 167.2 jit_solution(13272787207289847946)
XLA Ops:
  0.6 160.0 %shard_map.103 = (bf16[2,2,1536,768]{3,2,1,0:T(8,128)(2,1)S(1)}, f32[1536,768]{1,0:T(8,128)S(1)}, f32[1536,768]{1,0:T(8,128)S(1)}) custom-call(bf16[512,1536]{1,0:T(8,128)(2,1)} %gate.1, bf16[512,1536]{1,0:T(8,128)(2,1)} %up.1, bf16[512,3072]{1,0:T(8,128)(2,1)} %og.1, bf16[1536,3072]{1,0:T(8,128)(2,1)} %bitcast.6, f32[1536,768]{1,0:T(8,128)} %glob.1, ...), custom_call_target="tpu_custom_call" | custom-call | flops 9663676416 | bytes 103809024 | tf_op jit(solution)/shard_map/pallas_call | solution.py:424
  160.6 6.6 %shard_map.104 = (bf16[1536,3072]{1,0:T(8,128)(2,1)}, f32[1536,768]{1,0:T(8,128)}, f32[1536,768]{1,0:T(8,128)}) custom-call(bf16[2,2,1536,768]{3,2,1,0:T(8,128)(2,1)S(1)} %get-tuple-element.9.merged_v, f32[1536,768]{1,0:T(8,128)S(1)} %get-tuple-element.10.glob_v, f32[1536,768]{1,0:T(8,128)S(1)} %get-tuple-element.11.mom_v), custom_call_target="tpu_custom_call" | custom-call | bytes 18874368 | tf_op jit(solution)/shard_map/pallas_call | solution.py:473
